TPU v7x, 32 devices: a whole 2x2x4 slice. The times are simulated.
32 devices in a mesh: tgt: 4 (over z), src: 8 (over y, x, core).
Axes of the slice: x: 2, y: 2, z: 4, core: 2. Of those that a mesh axis runs over, the one named last changes fastest.
Arguments:
- target_xy: float32 [2, 2048], P(None, 'tgt'), may hold values from 0 to 20
- source_xy: float32 [2, 16384], P(None, 'src'), may hold values from 0 to 20
- body_of: int32 [16384], P('src'), may hold values from 0 to 127
- series_coef: float32 [2, 32, 128], replicated, may hold values from -2 to 2
- probe_matrix: bfloat16 [16384, 128], P('src'), may hold values from -0.046875 to 0.046875
- row_weight: float32 [2048], P('tgt'), may hold values from 1 to 36
Outputs:
- basis: float32 [2048, 256], P(('tgt', 'src'))
- factor: float32 [128, 128], replicated
All inputs are finite; a program needn't handle non-finite values.
Results may differ from a plain program's by a relative error of at most 0.0085.
Values sent between devices are 32-bit elements; how exact they have to be, the bound alone decides.
A program may use at most 64 MiB of HBM per device.

v0:
```python
import math

import jax
import jax.numpy as jnp
from jax import lax
from jax.sharding import PartitionSpec as P

NTERMS = 32


def swapped(array, axis, distance):
    return lax.ppermute(array, axis, [(i, i ^ 1 << distance) for i in range(lax.axis_size(axis))])


def panel_series(rows_xy, cols_xy, coef_re, coef_im):
    delta_x = rows_xy[0][:, None] - cols_xy[0][None, :]
    delta_y = rows_xy[1][:, None] - cols_xy[1][None, :]
    radius = jnp.sqrt(delta_x * delta_x + delta_y * delta_y + 0.25)
    decay_rate = jnp.exp(-0.005 * radius)
    step_re = decay_rate * jnp.cos(1.5 * radius)
    step_im = decay_rate * jnp.sin(1.5 * radius)
    term_count = coef_re.shape[0]
    total_re = jnp.broadcast_to(coef_re[term_count - 1][None, :], radius.shape)
    total_im = jnp.broadcast_to(coef_im[term_count - 1][None, :], radius.shape)
    for degree in range(term_count - 2, -1, -1):
        next_re = total_re * step_re - total_im * step_im + coef_re[degree][None, :]
        next_im = total_re * step_im + total_im * step_re + coef_im[degree][None, :]
        total_re, total_im = (next_re, next_im)
    series_re = total_re * step_re - total_im * step_im
    series_im = total_re * step_im + total_im * step_re
    tile_re = (1.0 / radius + series_re).astype(jnp.bfloat16)
    tile_im = series_im.astype(jnp.bfloat16)
    return (tile_re, tile_im)


def sketch_rows(target_xy, source_xy, picked, probe_matrix, row_count):
    source_count = probe_matrix.shape[0]
    block_width = math.gcd(source_count, 1024)
    blocks = source_count // block_width
    rank_width = probe_matrix.shape[1]

    def add_block(block_index, totals):
        block_start = block_index * block_width
        xy_block = lax.dynamic_slice_in_dim(source_xy, block_start, block_width, 1)
        coef_block = lax.dynamic_slice_in_dim(picked, block_start, block_width, 1)
        probe_block = lax.dynamic_slice_in_dim(probe_matrix, block_start, block_width, 0)
        tile_re, tile_im = panel_series(
            target_xy, xy_block, coef_block[:NTERMS], coef_block[NTERMS:]
        )
        part_re = jnp.dot(tile_re, probe_block, preferred_element_type=jnp.float32)
        part_im = jnp.dot(tile_im, probe_block, preferred_element_type=jnp.float32)
        return totals + jnp.concatenate([part_re, part_im], axis=1)

    start_totals = jnp.zeros((row_count, 2 * rank_width), jnp.float32)
    return lax.fori_loop(0, blocks, add_block, start_totals)


def gram_of(rows_part, scale_rows):
    rank_width = rows_part.shape[1] // 2
    stacked = rows_part.reshape(-1, rank_width)
    return jnp.dot(stacked.T, stacked, precision=lax.Precision.HIGHEST) / scale_rows


def outer_self(factor_part):
    return jnp.dot(factor_part, factor_part.T, precision=lax.Precision.HIGHEST)


def pick_coefficients(series_coef, body_of):
    bodies = series_coef.shape[2]
    one_hot = (jnp.arange(bodies, dtype=jnp.int32)[:, None] == body_of[None, :]).astype(
        jnp.bfloat16
    )
    table = series_coef.reshape(-1, bodies)
    high_part = table.astype(jnp.bfloat16)
    rest_one = table - high_part.astype(jnp.float32)
    middle_part = rest_one.astype(jnp.bfloat16)
    low_part = (rest_one - middle_part.astype(jnp.float32)).astype(jnp.bfloat16)
    picked = jnp.dot(high_part, one_hot, preferred_element_type=jnp.float32)
    picked = picked + jnp.dot(middle_part, one_hot, preferred_element_type=jnp.float32)
    return picked + jnp.dot(low_part, one_hot, preferred_element_type=jnp.float32)


def per_device(target_xy, source_xy, body_of, series_coef, probe_matrix, row_weight):
    rank_width = probe_matrix.shape[1]
    picked = pick_coefficients(series_coef, body_of)
    rows_all = target_xy.shape[1]
    own_count = rows_all // lax.axis_size("src")
    scale_rows = float(2 * rows_all * lax.axis_size("tgt"))
    own_start = lax.axis_index("src") * own_count
    partial_value = sketch_rows(target_xy, source_xy, picked, probe_matrix, rows_all)
    summed = lax.psum(partial_value, "src")
    weighted = summed * row_weight[:, None]
    gram_part = gram_of(weighted, scale_rows)
    own_rows = lax.dynamic_slice_in_dim(weighted, own_start, own_count, 0)
    lower_factor = jnp.linalg.cholesky(gram_part)
    for bit_index in range(lax.axis_size("tgt").bit_length() - 1):
        partner = swapped(lower_factor, "tgt", bit_index)
        lower_factor = jnp.linalg.cholesky(outer_self(lower_factor) + outer_self(partner))
    identity = jnp.eye(rank_width, dtype=jnp.float32)
    inverse = lax.linalg.triangular_solve(lower_factor, identity, left_side=True, lower=True)
    basis_rows = jnp.dot(
        own_rows.reshape(-1, rank_width), inverse.T, precision=lax.Precision.HIGHEST
    )
    return (basis_rows.reshape(own_count, 2 * rank_width), lower_factor.T)


def solution(mesh):
    return jax.shard_map(
        per_device,
        mesh=mesh,
        in_specs=(P(None, "tgt"), P(None, "src"), P("src"), P(), P("src", None), P("tgt")),
        out_specs=(P(("tgt", "src"), None), P()),
        check_vma=False,
    )
```

profile of v0, /device:TPU:0, one launch (start us, length us, event | category | flops | bytes accessed | tf_op | source)
XLA Modules:
  0.0 258.2 jit_solution(17578237345803980861)
XLA Ops:
  7.2 0.8 subtract_convert_fusion
  8.0 0.8 bitcast_convert_fusion
  8.8 1.0 convolution_bitcast_fusion
  11.2 117.8 %while.14 = (s32[]{:T(128)}, f32[512,256]{0,1:T(8,128)S(1)}, f32[2,512]{1,0:T(2,128)S(1)}, f32[2,2048]{1,0:T(2,128)S(1)}, f32[64,2048]{1,0:T(8,128)S(1)}, /*inde...) while((s32[]{:T(128)}, f32[512,256]{0,1:T(8,128)S(1)}, ...), condition=%wide.region_1.0_spmd.clone, body=%wide.region_0.0_spmd.clone.sunk | while | flops 544604224 | bytes 3720865 | solution.py:55
  12.2 26.8 %fusion.66 = f32[512,128]{0,1:T(8,128)S(1)} fusion(f32[1024]{0:T(1024)S(1)} %bitcast.361, f32[1024]{0:T(1024)S(1)} %bitcast.255, f32[1024]{0:T(1024)S(1)} %bitcast.257, f32[1024]{0:T(1024)S(1)} %bitcast.259, f32[1024]{0:T(1024)S(1)} %bitcast.261, f32[1024]{0:T(1024)S(1)} %bitcast.263, f32[1024]{0:T(1024)S(1)} %bitcast.265, f32[1024]{0:T(1024)S(1)} %bitcast.267, ...), kind=kOutput, calls=%fused_computation.69.clone.1 | convolution fusion | flops 272629760 | bytes 798724 | tf_op jit(solution)/shard_map/while/body/eval_jaxpr/dot_general | solution.py:50
  39.0 26.5 %fusion.65 = f32[512,128]{0,1:T(8,128)S(1)} fusion(f32[1024]{0:T(1024)S(1)} %bitcast.362, f32[1024]{0:T(1024)S(1)} %bitcast.256, f32[1024]{0:T(1024)S(1)} %bitcast.258, f32[1024]{0:T(1024)S(1)} %bitcast.260, f32[1024]{0:T(1024)S(1)} %bitcast.262, f32[1024]{0:T(1024)S(1)} %bitcast.264, f32[1024]{0:T(1024)S(1)} %bitcast.266, f32[1024]{0:T(1024)S(1)} %bitcast.268, ...), kind=kOutput, calls=%fused_computation.70.clone.1 | convolution fusion | flops 271581184 | bytes 798724 | tf_op jit(solution)/shard_map/while/body/eval_jaxpr/dot_general | solution.py:51
  66.8 26.8 %fusion.66 = f32[512,128]{0,1:T(8,128)S(1)} fusion(f32[1024]{0:T(1024)S(1)} %bitcast.361, f32[1024]{0:T(1024)S(1)} %bitcast.255, f32[1024]{0:T(1024)S(1)} %bitcast.257, f32[1024]{0:T(1024)S(1)} %bitcast.259, f32[1024]{0:T(1024)S(1)} %bitcast.261, f32[1024]{0:T(1024)S(1)} %bitcast.263, f32[1024]{0:T(1024)S(1)} %bitcast.265, f32[1024]{0:T(1024)S(1)} %bitcast.267, ...), kind=kOutput, calls=%fused_computation.69.clone.1 | convolution fusion | flops 272629760 | bytes 798724 | tf_op jit(solution)/shard_map/while/body/eval_jaxpr/dot_general | solution.py:50
  93.6 26.5 %fusion.65 = f32[512,128]{0,1:T(8,128)S(1)} fusion(f32[1024]{0:T(1024)S(1)} %bitcast.362, f32[1024]{0:T(1024)S(1)} %bitcast.256, f32[1024]{0:T(1024)S(1)} %bitcast.258, f32[1024]{0:T(1024)S(1)} %bitcast.260, f32[1024]{0:T(1024)S(1)} %bitcast.262, f32[1024]{0:T(1024)S(1)} %bitcast.264, f32[1024]{0:T(1024)S(1)} %bitcast.266, f32[1024]{0:T(1024)S(1)} %bitcast.268, ...), kind=kOutput, calls=%fused_computation.70.clone.1 | convolution fusion | flops 271581184 | bytes 798724 | tf_op jit(solution)/shard_map/while/body/eval_jaxpr/dot_general | solution.py:51
  129.0 0.8 copy-done
  129.8 57.4 %all-reduce.2.cloned.1.call-done = f32[512,256]{0,1:T(8,128)} async-done(((f32[512,256]{0,1:T(8,128)}), f32[512,256]{0,1:T(8,128)}) %all-reduce.2.cloned.1.call-update) | async-done | bytes 524304 | tf_op jit(solution)/shard_map/psum | solution.py:91
  187.2 1.1 broadcast_multiply_fusion
  188.6 1.0 convolution_multiply_fusion
  189.7 11.7 %cholesky.59 = f32[128,128]{1,0:T(8,128)S(1)} custom-call(f32[128,128]{1,0:T(8,128)S(1)} %fusion.21), custom_call_target="Cholesky" | custom-call | tf_op jit(solution)/shard_map/jit(cholesky)/cholesky | solution.py:95
  202.1 0.7 select_select_fusion.2
  202.8 1.5 collective-permute-start
  204.7 2.4 collective-permute-done
  207.5 11.7 %cholesky.70 = f32[128,128]{1,0:T(8,128)S(1)} custom-call(f32[128,128]{1,0:T(8,128)S(1)} %fusion.20), custom_call_target="Cholesky" | custom-call | tf_op jit(solution)/shard_map/jit(cholesky)/cholesky | solution.py:98
  219.9 0.7 select_select_fusion.1
  220.5 2.4 collective-permute-start.1
  223.2 2.6 collective-permute-done.1
  226.1 11.9 %cholesky.81 = f32[128,128]{1,0:T(8,128)S(1)} custom-call(f32[128,128]{1,0:T(8,128)S(1)} %fusion.19), custom_call_target="Cholesky" | custom-call | tf_op jit(solution)/shard_map/jit(cholesky)/cholesky | solution.py:98
  238.7 0.7 fusion.26
  239.4 9.8 %custom-call.5 = f32[1,128,128]{1,2,0:T(8,128)S(1)} custom-call(f32[1,128,128]{2,1,0:T(8,128)S(1)} %get-tuple-element.231), custom_call_target="InvertDiagBlocksLowerTriangular" | custom-call | tf_op jit(solution)/shard_map/triangular_solve | solution.py:100
  250.4 0.7 copy.27
  (52 shorter events, 8.8 us)
Async XLA Ops:
  7.2 2.6 %copy-start.3 = (s32[2048]{0:T(1024)S(1)}, s32[2048]{0:T(1024)}, u32[]{:S(2)}) copy-start(s32[2048]{0:T(1024)} %param.11) | copy-start | bytes 24580
  7.2 180.0 %all-reduce.2.cloned.1.call-start = ((), (), s32[]{:S(2)}) async-start(), calls=%async_computation | async-start | bytes 1048576 | tf_op jit(solution)/shard_map/psum | solution.py:91
  10.1 0.7 copy-start.1
  10.1 0.7 copy-start.2
  10.1 1.1 copy-start.5
  129.0 0.8 copy-start
  129.0 58.2 %copy-start.4 = (f32[512]{0:T(512)S(1)}, f32[512]{0:T(512)}, u32[]{:S(2)}) copy-start(f32[512]{0:T(512)} %param.14) | copy-start | bytes 6148
  202.8 4.3 %collective-permute-start = (f32[128,128]{1,0:T(8,128)S(1)}, f32[128,128]{1,0:T(8,128)S(1)}, u32[]{:S(2)}, u32[]{:S(2)}) collective-permute-start(f32[128,128]{1,0:T(8,128)S(1)} %select_select_fusion.2), channel_id=1, source_target_pairs={{0,8},{8,0},{16,24},{24,16},{1,9},{9,1},{17,25},{25,17},{2,10},{10... | collective-permute-start | bytes 196616 | tf_op jit(solution)/shard_map/ppermute | solution.py:12
  220.5 5.2 %collective-permute-start.1 = (f32[128,128]{1,0:T(8,128)S(1)}, f32[128,128]{1,0:T(8,128)S(1)}, u32[]{:S(2)}, u32[]{:S(2)}) collective-permute-start(f32[128,128]{1,0:T(8,128)S(1)} %select_select_fusion.1), channel_id=1, source_target_pairs={{0,16},{8,24},{16,0},{24,8},{1,17},{9,25},{17,1},{25,9},{2,18},{10... | collective-permute-start | bytes 196616 | tf_op jit(solution)/shard_map/ppermute | solution.py:12
Sparse Core Ops, SparseCore 0:
  130.0 57.2 all-reduce.1
where the time goes:
time: 259 us; the launch traced here: 258 us
  matrix products  111 us (43%)
  waiting for transfers between devices  62.4 us (24%)
  other arithmetic  52.2 us (20%)
  between operations  14.5 us (6%)
  loops' own time  8.82 us (3%)
  local copies, waits for them, and re-layouts  5.63 us (2%)
  starting transfers between devices  3.92 us (2%)
    psum x1, waiting for transfers between devices, per_device(): summed = lax.psum(partial_value, 'src')  57.4 us
    dot_general x2, matrix products, add_block(): part_re = jnp.dot(tile_re, probe_block, preferred_element_type=jnp.float32)  53.5 us
    dot_general x2, matrix products, add_block(): part_im = jnp.dot(tile_im, probe_block, preferred_element_type=jnp.float32)  53.1 us
    another operation x6, other arithmetic, per_device(): jnp.linalg.cholesky(outer_self(lower_factor) + outer_self(partner))  25 us
    another operation x3, other arithmetic, per_device(): lower_factor = jnp.linalg.cholesky(gram_part)  12.4 us
    another operation x1, other arithmetic, per_device(): lax.linalg.triangular_solve(lower_factor, identity, left_side=True, lower...  9.81 us
    another operation x1, loops' own time, sketch_rows(): return lax.fori_loop(0, blocks, add_block, start_totals)  8.82 us
  transfers between devices with their start and end apart: 3, of which 3 were waited for; matrix products, arithmetic and copies ran while one was open for 0% of the time, Pallas kernels for 0%

commit v1 on v0

v1 whole, which is shorter than its diff:
```python
import functools
import math

import jax
import jax.numpy as jnp
from jax import lax
from jax.experimental import pallas as pl
from jax.experimental.pallas import tpu as pltpu
from jax.sharding import PartitionSpec as P

LANES = 128
TURNS = 1.5 / (2.0 * math.pi)
ROUNDER = 12582912.0
SIN_TERMS = (1.570796322, -0.6459634782, 0.07968022286, -0.004602163105)
COS_TERMS = (0.9999999724, -1.233697011, 0.2535986077, -0.02040825547)


def horner(terms, point):
    total = terms[-1]
    for term in terms[-2::-1]:
        total = total * point + term
    return total


def wave_step(tx, ty, sx, sy):
    delta_x = tx - sx
    delta_y = ty - sy
    squared = delta_x * delta_x + delta_y * delta_y + 0.25
    inverse = lax.rsqrt(squared)
    radius = squared * inverse
    radius = radius + (0.5 * inverse) * (squared - radius * radius)
    turns = radius * TURNS
    part = turns - ((turns + ROUNDER) - ROUNDER)
    point = part * part
    sine = horner(SIN_TERMS, point) * part
    cosine = horner(COS_TERMS, point)
    for _ in range(2):
        sine, cosine = 2.0 * sine * cosine, 1.0 - 2.0 * sine * sine
    decay = jnp.exp(-0.005 * radius)
    return inverse, decay * cosine, decay * sine


def spread_rows(row):
    return jnp.transpose(jnp.broadcast_to(row, (LANES, LANES)))


def pick_coefficients(coef, bodies):
    count = coef.shape[1]
    one_hot = (
        lax.broadcasted_iota(jnp.int32, (count, bodies.shape[1]), 0) == bodies
    ).astype(jnp.float32).astype(jnp.bfloat16)
    picked = None
    rest = coef
    for _ in range(3):
        part = rest.astype(jnp.bfloat16)
        rest = rest - part.astype(jnp.float32)
        term = jnp.dot(part, one_hot, preferred_element_type=jnp.float32)
        picked = term if picked is None else picked + term
    return picked


def sketch_kernel(row_block, width, txy, sxy, body, coef, probe, out, spread, picked):
    rows = txy.shape[1]
    sources = sxy.shape[1]
    terms = coef.shape[0] // 2
    blocks = sources // width
    for axis in range(2):
        for start in range(0, rows, LANES):
            spread[axis, start : start + LANES, :] = spread_rows(
                txy[axis : axis + 1, start : start + LANES]
            )

    def pick(block, carry):
        at = pl.ds(pl.multiple_of(block * width, width), width)
        picked[:, at] = pick_coefficients(coef[...], body[:, at])
        return carry

    lax.fori_loop(0, blocks, pick, 0)

    def half(row_at, start):
        at = pl.ds(pl.multiple_of(start, LANES), LANES)
        inverse, step_re, step_im = wave_step(
            spread[0, row_at, :], spread[1, row_at, :], sxy[0:1, at], sxy[1:2, at]
        )

        def term(index):
            return picked[index : index + 1, at]

        total_re, total_im = term(terms - 1), term(2 * terms - 1)
        for degree in range(terms - 2, -1, -1):
            total_re, total_im = (
                (total_re * step_re - total_im * step_im) + term(degree),
                (total_re * step_im + total_im * step_re) + term(terms + degree),
            )
        series_re = total_re * step_re - total_im * step_im
        series_im = total_re * step_im + total_im * step_re
        return (inverse + series_re).astype(jnp.bfloat16), series_im.astype(jnp.bfloat16)

    def tile(row_at, block):
        halves = [half(row_at, block * width + start) for start in range(0, width, LANES)]
        return jnp.concatenate(
            [jnp.concatenate([h[0] for h in halves], axis=1),
             jnp.concatenate([h[1] for h in halves], axis=1)], axis=0)

    def product(held, block):
        at = pl.ds(pl.multiple_of(block * width, width), width)
        return jnp.dot(held, probe[at, :], preferred_element_type=jnp.float32)

    def chunk(index, carry):
        row_at = pl.ds(pl.multiple_of(index * row_block, row_block), row_block)

        def step(block, state):
            held, total = state
            total = total + product(held, block - 1)
            return tile(row_at, block), total

        zero = jnp.zeros((2 * row_block, LANES), jnp.float32)
        held, total = lax.fori_loop(1, blocks, step, (tile(row_at, 0), zero))
        total = total + product(held, blocks - 1)
        out[row_at, :LANES] = total[:row_block]
        out[row_at, LANES:] = total[row_block:]
        return carry

    lax.fori_loop(0, rows // row_block, chunk, 0)


def sketch(target_xy, source_xy, body_of, series_coef, probe_matrix):
    rows = target_xy.shape[1]
    sources = source_xy.shape[1]
    table = series_coef.reshape(-1, series_coef.shape[2])
    return pl.pallas_call(
        functools.partial(sketch_kernel, math.gcd(rows, 64), 2 * LANES),
        out_shape=jax.ShapeDtypeStruct((rows, 2 * probe_matrix.shape[1]), jnp.float32),
        in_specs=[pl.BlockSpec(memory_space=pltpu.VMEM)] * 5,
        out_specs=pl.BlockSpec(memory_space=pltpu.VMEM),
        scratch_shapes=[
            pltpu.VMEM((2, rows, LANES), jnp.float32),
            pltpu.VMEM((table.shape[0], sources), jnp.float32),
        ],
        compiler_params=pltpu.CompilerParams(vmem_limit_bytes=32 * 1024 * 1024),
        name="sketch",
    )(target_xy, source_xy, body_of[None, :], table, probe_matrix)


def per_device(target_xy, source_xy, body_of, series_coef, probe_matrix, row_weight):
    rank_width = probe_matrix.shape[1]
    rows_all = target_xy.shape[1]
    own_count = rows_all // lax.axis_size("src")
    scale_rows = float(2 * rows_all * lax.axis_size("tgt"))
    own_start = lax.axis_index("src") * own_count
    partial_value = sketch(target_xy, source_xy, body_of, series_coef, probe_matrix)
    own_rows = lax.psum_scatter(partial_value, "src", scatter_dimension=0, tiled=True)
    own_weight = lax.dynamic_slice_in_dim(row_weight, own_start, own_count, 0)
    stacked = (own_rows * own_weight[:, None]).reshape(-1, rank_width)
    gram = jnp.dot(stacked.T, stacked, precision=lax.Precision.HIGHEST)
    gram = lax.psum(gram, ("tgt", "src")) / scale_rows
    lower_factor = jnp.linalg.cholesky(gram)
    identity = jnp.eye(rank_width, dtype=jnp.float32)
    inverse = lax.linalg.triangular_solve(lower_factor, identity, left_side=True, lower=True)
    basis_rows = jnp.dot(stacked, inverse.T, precision=lax.Precision.HIGHEST)
    return (basis_rows.reshape(own_count, 2 * rank_width), lower_factor.T)


def solution(mesh):
    return jax.shard_map(
        per_device,
        mesh=mesh,
        in_specs=(P(None, "tgt"), P(None, "src"), P("src"), P(), P("src", None), P("tgt")),
        out_specs=(P(("tgt", "src"), None), P()),
        check_vma=False,
    )
```

time: 259 us -> 254 us (0.981)
  matrix products: 111 us -> 1.44 us
  waiting for transfers between devices: 62.4 us -> 159 us
  Pallas kernels: 0 us -> 46.4 us
  other arithmetic: 52.2 us -> 24.6 us
  loops' own time: 8.82 us -> 0 us
  starting transfers between devices: 3.92 us -> 0.08 us
    dot_general x13 -> x2, matrix products: 111 us -> 1.19 us  [the longest x1 0.92 us: per_device(): gram = jnp.dot(stacked.T, stacked, precision=lax.Precision.HIGHEST)]
    psum x1, waiting for transfers between devices: 57.4 us -> 123 us  [per_device(): gram = lax.psum(gram, ('tgt', 'src')) / scale_rows]
    pallas_call x0 -> x1, Pallas kernels: none -> 46.4 us  [sketch(): pl.pallas_call(functools.partial(sketch_kernel, math.gcd(rows, 64), 2 * L...]
    reduce_scatter x0 -> x1, waiting for transfers between devices: none -> 36.1 us  [per_device(): lax.psum_scatter(partial_value, 'src', scatter_dimension=0, tiled=True)]
    another operation x9 -> x3, other arithmetic: 37.4 us -> 12.4 us  [per_device(): lower_factor = jnp.linalg.cholesky(gram)]
    another operation x1 -> x0, loops' own time: 8.82 us -> none  [sketch_rows(): return lax.fori_loop(0, blocks, add_block, start_totals)]
    ppermute x2 -> x0, waiting for transfers between devices: 4.95 us -> none  [swapped(): lax.ppermute(array, axis, [(i, i ^ 1 << distance) for i in range(lax.axis...]
    ppermute x2 -> x0, starting transfers between devices: 3.88 us -> none  [swapped(): lax.ppermute(array, axis, [(i, i ^ 1 << distance) for i in range(lax.axis...]
  transfers between devices with their start and end apart: 3 -> 2, of which waited for: 3 -> 2; matrix products, arithmetic and copies ran while one was open for 0% -> 0% of each run, Pallas kernels for 0% -> 0%
where the time goes in v1:
time: 254 us; the launch traced here: 252 us
  waiting for transfers between devices  159 us (63%)
  Pallas kernels  46.4 us (18%)
  other arithmetic  24.6 us (10%)
  between operations  14.1 us (6%)
  local copies, waits for them, and re-layouts  6.87 us (3%)
    psum x1, waiting for transfers between devices, per_device(): gram = lax.psum(gram, ('tgt', 'src')) / scale_rows  123 us
    pallas_call x1, Pallas kernels, sketch(): pl.pallas_call(functools.partial(sketch_kernel, math.gcd(rows, 64), 2 * L...  46.4 us
    reduce_scatter x1, waiting for transfers between devices, per_device(): lax.psum_scatter(partial_value, 'src', scatter_dimension=0, tiled=True)  36.1 us
    another operation x3, other arithmetic, per_device(): lower_factor = jnp.linalg.cholesky(gram)  12.4 us
    another operation x1, other arithmetic, per_device(): lax.linalg.triangular_solve(lower_factor, identity, left_side=True, lower...  9.81 us
    unnamed x13, local copies, waits for them, and re-layouts  5.36 us
  transfers between devices with their start and end apart: 2, of which 2 were waited for; matrix products, arithmetic and copies ran while one was open for 0% of the time, Pallas kernels for 0%

profile of v1, /device:TPU:0, one launch (start us, length us, event | category | flops | bytes accessed | tf_op | source)
XLA Modules:
  0.0 252.4 jit_solution(8931038463702757590)
XLA Ops:
  7.2 0.0 reduce-scatter.2.cloned.1.call-start
  7.2 1.0 copy-done
  8.3 0.8 copy-done.1
  9.0 0.7 copy-done.2
  9.7 0.7 copy-done.3
  10.4 0.7 copy-done.4
  11.1 46.4 %sketch.1 = f32[512,256]{1,0:T(8,128)} custom-call(f32[2,512]{1,0:T(2,128)S(1)} %copy-done.4, f32[2,2048]{1,0:T(2,128)S(1)} %copy-done.2, s32[1,2048]{1,0:T(1,128)S(1)} %bitcast.18, f32[64,128]{1,0:T(8,128)S(1)} %bitcast.17, bf16[2048,128]{1,0:T(8,128)(2,1)S(1)} %copy-done), custom_call_target="tpu_custom_call" | custom-call | tf_op jit(solution)/shard_map/sketch/pallas_call | solution.py:131
  57.5 0.0 all-reduce.2.cloned.1.call-start
  57.6 0.8 dynamic_slice.3
  58.4 36.1 %reduce-scatter.2.cloned.1.call-done = f32[64,256]{1,0:T(8,128)} async-done(((f32[512,256]{1,0:T(8,128)}), f32[64,256]{1,0:T(8,128)}) %reduce-scatter.2.cloned.1.call-update) | async-done | bytes 65552 | tf_op jit(solution)/shard_map/reduce_scatter | solution.py:152
  94.5 0.9 broadcast_multiply_fusion.1
  95.4 0.9 fusion.4
  96.4 122.8 %all-reduce.2.cloned.1.call-done = f32[128,128]{0,1:T(8,128)} async-done(((f32[128,128]{0,1:T(8,128)}), f32[128,128]{0,1:T(8,128)}) %all-reduce.2.cloned.1.call-update) | async-done | bytes 65552 | tf_op jit(solution)/shard_map/psum | solution.py:156
  219.1 0.8 broadcast_multiply_fusion
  220.0 0.1 copy.9
  220.1 0.7 copy-done.5
  220.8 11.7 %cholesky.17 = f32[128,128]{1,0:T(8,128)S(1)} custom-call(f32[128,128]{1,0:T(8,128)S(1)} %fusion.2), custom_call_target="Cholesky" | custom-call | tf_op jit(solution)/shard_map/jit(cholesky)/cholesky | solution.py:157
  232.6 0.6 compare_reduce_fusion
  233.2 0.7 fusion.3
  233.9 9.8 %custom-call.6 = f32[1,128,128]{1,2,0:T(8,128)S(1)} custom-call(f32[1,128,128]{2,1,0:T(8,128)S(1)} %get-tuple-element.5), custom_call_target="InvertDiagBlocksLowerTriangular" | custom-call | tf_op jit(solution)/shard_map/triangular_solve | solution.py:159
  243.7 0.2 fusion
  244.0 0.3 fusion.5
  244.2 0.7 reshape.25
  244.9 0.7 copy.10
  (11 shorter events, 0.1 us)
Async XLA Ops:
  7.2 87.3 %reduce-scatter.2.cloned.1.call-start = ((), (), s32[]{:S(2)}) async-start(), calls=%async_computation.1 | async-start | bytes 589824 | tf_op jit(solution)/shard_map/reduce_scatter | solution.py:152
  7.2 1.0 copy-start
  8.3 0.8 copy-start.1
  9.0 0.7 copy-start.2
  9.7 0.7 copy-start.3
  10.4 0.7 copy-start.4
  57.5 161.6 %all-reduce.2.cloned.1.call-start = ((), (), s32[]{:S(2)}) async-start(), calls=%async_computation.2 | async-start | bytes 131072 | tf_op jit(solution)/shard_map/psum | solution.py:156
  220.0 0.8 copy-start.5
Sparse Core Ops, SparseCore 0:
  57.7 36.7 reduce-scatter.1
  101.6 117.5 all-reduce.1

commit v2 on v1

--- a/solution.py
+++ b/solution.py
@@ -59,16 +59,70 @@
     return picked
 
 
-def sketch_kernel(row_block, width, txy, sxy, body, coef, probe, out, spread, picked):
+def remote(source, target, send_sem, recv_sem, axis, peer):
+    return pltpu.make_async_remote_copy(
+        src_ref=source,
+        dst_ref=target,
+        send_sem=send_sem,
+        recv_sem=recv_sem,
+        device_id={axis: peer},
+        device_id_type=pl.DeviceIdType.MESH,
+    )
+
+
+def guarded(condition, needed, action):
+    if needed:
+        pl.when(condition)(action)
+    else:
+        action()
+
+
+def sketch_kernel(
+    row_block, width, n_src, n_tgt, scale,
+    txy_in, sxy_in, body_in, coef_in, probe_in, weight_in, stacked_out, gram_out,
+    txy, sxy, body, coef, probe, weight, spread, picked, sums, landed,
+    gram_mine, gram_landed, piece_mine, piece_landed, gram_full,
+    in_sem, row_send, row_recv, gram_send, gram_recv, tgt_send, tgt_recv, all_send, all_recv,
+):
+    src_me = lax.axis_index("src")
+    tgt_me = lax.axis_index("tgt")
+    src_peers = [lax.rem(src_me + offset, n_src) for offset in range(1, n_src)]
+    tgt_peers = [lax.rem(tgt_me + offset, n_tgt) for offset in range(1, n_tgt)]
+    barrier = pltpu.get_barrier_semaphore()
+    for axis, peers in (("src", src_peers), ("tgt", tgt_peers)):
+        for peer in peers:
+            pl.semaphore_signal(
+                barrier, inc=1, device_id={axis: peer}, device_id_type=pl.DeviceIdType.MESH
+            )
+
+    loads = [
+        pltpu.make_async_copy(start, end, in_sem.at[index])
+        for index, (start, end) in enumerate(
+            ((txy_in, txy), (sxy_in, sxy), (body_in, body), (coef_in, coef),
+             (weight_in, weight), (probe_in, probe))
+        )
+    ]
+    for load in loads:
+        load.start()
+    for load in loads:
+        load.wait()
+
     rows = txy.shape[1]
     sources = sxy.shape[1]
     terms = coef.shape[0] // 2
     blocks = sources // width
-    for axis in range(2):
+    own = rows // n_src
+    chunks = rows // row_block
+    owners_in = row_block // own
+    rank_width = probe.shape[1]
+    piece = piece_mine.shape[0]
+    owners = rank_width // piece
+
+    for axis in range(3):
         for start in range(0, rows, LANES):
-            spread[axis, start : start + LANES, :] = spread_rows(
-                txy[axis : axis + 1, start : start + LANES]
-            )
+            at = slice(start, start + LANES)
+            row = weight[0:1, at] if axis == 2 else txy[axis : axis + 1, at]
+            spread[axis, at, :] = spread_rows(row)
 
     def pick(block, carry):
         at = pl.ds(pl.multiple_of(block * width, width), width)
@@ -106,7 +160,11 @@
         at = pl.ds(pl.multiple_of(block * width, width), width)
         return jnp.dot(held, probe[at, :], preferred_element_type=jnp.float32)
 
-    def chunk(index, carry):
+    def owned(owner):
+        return sums.at[pl.ds(pl.multiple_of(owner * own, own), own), :]
+
+    def chunk(turn, carry):
+        index = lax.rem(turn + 1 + src_me // owners_in, chunks)
         row_at = pl.ds(pl.multiple_of(index * row_block, row_block), row_block)
 
         def step(block, state):
@@ -117,48 +175,199 @@
         zero = jnp.zeros((2 * row_block, LANES), jnp.float32)
         held, total = lax.fori_loop(1, blocks, step, (tile(row_at, 0), zero))
         total = total + product(held, blocks - 1)
-        out[row_at, :LANES] = total[:row_block]
-        out[row_at, LANES:] = total[row_block:]
+        sums[row_at, :LANES] = total[:row_block]
+        sums[row_at, LANES:] = total[row_block:]
+
+        @pl.when(turn == 0)
+        def _():
+            pl.semaphore_wait(barrier, len(src_peers) + len(tgt_peers))
+
+        for inner in range(owners_in):
+            owner = index * owners_in + inner
+
+            @pl.when(owner != src_me)
+            def _():
+                remote(owned(owner), landed.at[src_me], row_send.at[owner], row_recv.at[src_me],
+                       "src", owner).start()
+
         return carry
 
-    lax.fori_loop(0, rows // row_block, chunk, 0)
-
-
-def sketch(target_xy, source_xy, body_of, series_coef, probe_matrix):
+    lax.fori_loop(0, chunks, chunk, 0)
+
+    own_at = pl.ds(pl.multiple_of(src_me * own, own), own)
+    landed[src_me] = sums[own_at, :]
+    for peer in src_peers:
+        remote(owned(peer), landed.at[peer], row_send.at[peer], row_recv.at[peer],
+               "src", peer).wait()
+    total = landed[0]
+    for sender in range(1, n_src):
+        total = total + landed[sender]
+    own_weight = spread[2, own_at, :]
+    stacked = jnp.concatenate(
+        [total[:, :rank_width] * own_weight, total[:, rank_width:] * own_weight], axis=0)
+    stacked_out[...] = stacked
+    gram_mine[...] = lax.dot_general(
+        stacked, stacked, (((0,), (0,)), ((), ())),
+        precision=lax.Precision.HIGHEST, preferred_element_type=jnp.float32)
+
+    def part_of(ref, owner):
+        return ref.at[pl.ds(pl.multiple_of(owner * piece, piece), piece), :]
+
+    some_idle = owners < n_src
+    mine = src_me < owners
+    for peer in src_peers:
+        guarded(peer < owners, some_idle, lambda peer=peer: remote(
+            part_of(gram_mine, peer), gram_landed.at[src_me], gram_send.at[peer],
+            gram_recv.at[src_me], "src", peer).start())
+
+    def merge():
+        at = pl.ds(pl.multiple_of(src_me * piece, piece), piece)
+        gram_landed[src_me] = gram_mine[at, :]
+        for peer in src_peers:
+            remote(part_of(gram_mine, src_me), gram_landed.at[peer], gram_send.at[peer],
+                   gram_recv.at[peer], "src", peer).wait_recv()
+        merged = gram_landed[0]
+        for sender in range(1, n_src):
+            merged = merged + gram_landed[sender]
+        piece_mine[...] = merged
+        copies = [remote(piece_mine, piece_landed.at[tgt_me], tgt_send.at[peer],
+                         tgt_recv.at[tgt_me], "tgt", peer) for peer in tgt_peers]
+        for copy in copies:
+            copy.start()
+        piece_landed[tgt_me] = merged
+        for peer in tgt_peers:
+            remote(piece_mine, piece_landed.at[peer], tgt_send.at[peer],
+                   tgt_recv.at[peer], "tgt", peer).wait_recv()
+        whole = piece_landed[0]
+        for sender in range(1, n_tgt):
+            whole = whole + piece_landed[sender]
+        gram_full[at, :] = whole * scale
+        sends = [remote(part_of(gram_full, src_me), part_of(gram_full, src_me),
+                        all_send.at[peer], all_recv.at[src_me], "src", peer)
+                 for peer in src_peers]
+        for copy in sends:
+            copy.start()
+        for copy in copies + sends:
+            copy.wait_send()
+
+    guarded(mine, some_idle, merge)
+    for peer in src_peers:
+        guarded(peer < owners, some_idle, lambda peer=peer: remote(
+            part_of(gram_mine, peer), part_of(gram_full, peer), gram_send.at[peer],
+            all_recv.at[peer], "src", peer).wait())
+    gram_out[...] = gram_full[...]
+
+
+def sketch(target_xy, source_xy, body_of, series_coef, probe_matrix, row_weight):
     rows = target_xy.shape[1]
-    sources = source_xy.shape[1]
+    sources, rank_width = probe_matrix.shape
+    n_src = lax.axis_size("src")
+    n_tgt = lax.axis_size("tgt")
+    own = rows // n_src
     table = series_coef.reshape(-1, series_coef.shape[2])
+    inputs = (target_xy, source_xy, body_of[None, :], table, probe_matrix, row_weight[None, :])
+    piece = max(8, rank_width // n_src)
+    dma = pltpu.SemaphoreType.DMA
+    held = [pltpu.VMEM(inputs[i].shape, inputs[i].dtype) for i in range(6)]
+    scale = 1.0 / (2.0 * rows * n_tgt)
     return pl.pallas_call(
-        functools.partial(sketch_kernel, math.gcd(rows, 64), 2 * LANES),
-        out_shape=jax.ShapeDtypeStruct((rows, 2 * probe_matrix.shape[1]), jnp.float32),
-        in_specs=[pl.BlockSpec(memory_space=pltpu.VMEM)] * 5,
-        out_specs=pl.BlockSpec(memory_space=pltpu.VMEM),
+        functools.partial(sketch_kernel, max(own, math.gcd(rows, 64)), 2 * LANES, n_src, n_tgt, scale),
+        out_shape=(
+            jax.ShapeDtypeStruct((2 * own, rank_width), jnp.float32),
+            jax.ShapeDtypeStruct((rank_width, rank_width), jnp.float32),
+        ),
+        in_specs=[pl.BlockSpec(memory_space=pl.ANY)] * 6,
+        out_specs=[pl.BlockSpec(memory_space=pltpu.VMEM)] * 2,
+        scratch_shapes=held + [
+            pltpu.VMEM((3, rows, LANES), jnp.float32),
+            pltpu.VMEM((table.shape[0], sources), jnp.float32),
+            pltpu.VMEM((rows, 2 * rank_width), jnp.float32),
+            pltpu.VMEM((n_src, own, 2 * rank_width), jnp.float32),
+            pltpu.VMEM((rank_width, rank_width), jnp.float32),
+            pltpu.VMEM((n_src, piece, rank_width), jnp.float32),
+            pltpu.VMEM((piece, rank_width), jnp.float32),
+            pltpu.VMEM((n_tgt, piece, rank_width), jnp.float32),
+            pltpu.VMEM((rank_width, rank_width), jnp.float32),
+            dma((6,)), dma((n_src,)), dma((n_src,)), dma((n_src,)), dma((n_src,)),
+            dma((n_tgt,)), dma((n_tgt,)), dma((n_src,)), dma((n_src,)),
+        ],
+        compiler_params=pltpu.CompilerParams(
+            collective_id=0, has_side_effects=True, vmem_limit_bytes=60 * 1024 * 1024
+        ),
+        name="sketch",
+    )(*inputs)
+
+
+def factor_kernel(own, stacked, gram, basis, factor, work, inverse):
+    size = gram.shape[0]
+    rows_at = lax.broadcasted_iota(jnp.int32, (size, size), 0)
+    columns_at = lax.broadcasted_iota(jnp.int32, (size, size), 1)
+    work[:, :size] = gram[...]
+    work[:, size:] = jnp.where(rows_at == columns_at, 1.0, 0.0)
+    depth = 8
+    sub = lax.broadcasted_iota(jnp.int32, (depth, size), 0)
+
+    def row_of(block, index):
+        return jnp.broadcast_to(block[index : index + 1, :], (depth, size))
+
+    for start in range(0, size, depth):
+        end = start + depth
+        left = work[start:end, :size]
+        right = work[start:end, size:]
+        columns = [
+            jnp.broadcast_to(left[:, start + c : start + c + 1], (depth, size))
+            for c in range(depth)
+        ]
+        pivots = None
+        for k in range(depth):
+            pivot = row_of(columns[k], k)
+            pivots = pivot if pivots is None else jnp.where(sub >= k, pivot, pivots)
+            if k == depth - 1:
+                break
+            ratio = jnp.where(sub > k, columns[k] / pivot, 0.0)
+            for c in range(k + 1, depth):
+                columns[c] = columns[c] - ratio * row_of(columns[c], k)
+            left = left - ratio * row_of(left, k)
+            right = right - ratio * row_of(right, k)
+        gain = 1.0 / jnp.sqrt(pivots)
+        left = left * gain
+        right = right * gain
+        left = jnp.where(columns_at[:depth] >= start + sub, left, 0.0)
+        factor[start:end, :] = left
+        inverse[start:end, :] = right
+        if end < size:
+            both = jnp.concatenate([left, right], axis=1)
+            work[end:, :] = work[end:, :] - lax.dot_general(
+                left[:, end:], both, (((0,), (0,)), ((), ())),
+                precision=lax.Precision.HIGHEST, preferred_element_type=jnp.float32)
+    result = lax.dot_general(
+        stacked[...], inverse[...], (((1,), (1,)), ((), ())),
+        precision=lax.Precision.HIGHEST, preferred_element_type=jnp.float32)
+    basis[:, :size] = result[:own]
+    basis[:, size:] = result[own:]
+
+
+def orthonormalize(stacked, gram):
+    size = gram.shape[0]
+    own = stacked.shape[0] // 2
+    return pl.pallas_call(
+        functools.partial(factor_kernel, own),
+        out_shape=(
+            jax.ShapeDtypeStruct((own, 2 * size), jnp.float32),
+            jax.ShapeDtypeStruct((size, size), jnp.float32),
+        ),
+        in_specs=[pl.BlockSpec(memory_space=pltpu.VMEM)] * 2,
+        out_specs=[pl.BlockSpec(memory_space=pltpu.VMEM)] * 2,
         scratch_shapes=[
-            pltpu.VMEM((2, rows, LANES), jnp.float32),
-            pltpu.VMEM((table.shape[0], sources), jnp.float32),
+            pltpu.VMEM((size, 2 * size), jnp.float32),
+            pltpu.VMEM((size, size), jnp.float32),
         ],
-        compiler_params=pltpu.CompilerParams(vmem_limit_bytes=32 * 1024 * 1024),
-        name="sketch",
-    )(target_xy, source_xy, body_of[None, :], table, probe_matrix)
-
-
-def per_device(target_xy, source_xy, body_of, series_coef, probe_matrix, row_weight):
-    rank_width = probe_matrix.shape[1]
-    rows_all = target_xy.shape[1]
-    own_count = rows_all // lax.axis_size("src")
-    scale_rows = float(2 * rows_all * lax.axis_size("tgt"))
-    own_start = lax.axis_index("src") * own_count
-    partial_value = sketch(target_xy, source_xy, body_of, series_coef, probe_matrix)
-    own_rows = lax.psum_scatter(partial_value, "src", scatter_dimension=0, tiled=True)
-    own_weight = lax.dynamic_slice_in_dim(row_weight, own_start, own_count, 0)
-    stacked = (own_rows * own_weight[:, None]).reshape(-1, rank_width)
-    gram = jnp.dot(stacked.T, stacked, precision=lax.Precision.HIGHEST)
-    gram = lax.psum(gram, ("tgt", "src")) / scale_rows
-    lower_factor = jnp.linalg.cholesky(gram)
-    identity = jnp.eye(rank_width, dtype=jnp.float32)
-    inverse = lax.linalg.triangular_solve(lower_factor, identity, left_side=True, lower=True)
-    basis_rows = jnp.dot(stacked, inverse.T, precision=lax.Precision.HIGHEST)
-    return (basis_rows.reshape(own_count, 2 * rank_width), lower_factor.T)
+        name="orthonormalize",
+    )(stacked, gram)
+
+
+def per_device(*arguments):
+    return orthonormalize(*sketch(*arguments))
 
 
 def solution(mesh):

time: 254 us -> 72.6 us (0.29)
  waiting for transfers between devices: 159 us -> 0 us
  Pallas kernels: 46.4 us -> 71.8 us
  other arithmetic: 24.6 us -> 0 us
  between operations: 14.1 us -> 0.64 us
  local copies, waits for them, and re-layouts: 6.87 us -> 0 us
    psum x1 -> x0, waiting for transfers between devices: 123 us -> none  [per_device(): gram = lax.psum(gram, ('tgt', 'src')) / scale_rows]
    reduce_scatter x1 -> x0, waiting for transfers between devices: 36.1 us -> none  [per_device(): lax.psum_scatter(partial_value, 'src', scatter_dimension=0, tiled=True)]
    pallas_call x1 -> x2, Pallas kernels: 46.4 us -> 71.8 us  [the longest x1 61.9 us: sketch(): pl.pallas_call(functools.partial(sketch_kernel, max(own, math.gcd(rows, 6...]
    another operation x4 -> x0, other arithmetic: 22.2 us -> none  [the longest x3 12.4 us: per_device(): lower_factor = jnp.linalg.cholesky(gram)]
    unnamed x13 -> x0, local copies, waits for them, and re-layouts: 5.36 us -> none
  transfers between devices with their start and end apart: 2 -> 0, of which waited for: 2 -> 0; matrix products, arithmetic and copies ran while one was open for 0% -> 0% of each run, Pallas kernels for 0% -> 0%
where the time goes in v2:
time: 72.6 us; the launch traced here: 72.4 us
  Pallas kernels  71.8 us (99%)
    pallas_call x1, Pallas kernels, sketch(): pl.pallas_call(functools.partial(sketch_kernel, max(own, math.gcd(rows, 6...  61.9 us
    pallas_call x1, Pallas kernels, orthonormalize(): pl.pallas_call(functools.partial(factor_kernel, own), out_shape=(jax.Shap...  9.93 us

profile of v2, /device:TPU:0, one launch (start us, length us, event | category | flops | bytes accessed | tf_op | source)
XLA Modules:
  0.0 72.4 jit_solution(14786632550650215675)
XLA Ops:
  0.6 61.9 %sketch.1 = (f32[128,128]{1,0:T(8,128)}, f32[128,128]{1,0:T(8,128)}) custom-call(f32[2,512]{1,0:T(2,128)} %txy_in.1, f32[2,2048]{1,0:T(2,128)} %sxy_in.1, s32[1,2048]{1,0:T(1,128)} %bitcast.4, f32[64,128]{1,0:T(8,128)} %bitcast.3, bf16[2048,128]{1,0:T(8,128)(2,1)} %probe_in.1, f32[1,512]{1,0:T(1,128)} %bitcast.5), custom_call_target="tpu_custom_call" | custom-call | tf_op jit(solution)/shard_map/sketch/pallas_call | solution.py:273
  62.5 9.9 %orthonormalize.1 = (f32[64,256]{1,0:T(8,128)}, f32[128,128]{1,0:T(8,128)}) custom-call(f32[128,128]{1,0:T(8,128)} %get-tuple-element.4.stacked, f32[128,128]{1,0:T(8,128)} %get-tuple-element.5.gram), custom_call_target="tpu_custom_call" | custom-call | tf_op jit(solution)/shard_map/orthonormalize/pallas_call | solution.py:353

commit v3 on v2

--- a/solution.py
+++ b/solution.py
@@ -35,8 +35,9 @@
     sine = horner(SIN_TERMS, point) * part
     cosine = horner(COS_TERMS, point)
     for _ in range(2):
-        sine, cosine = 2.0 * sine * cosine, 1.0 - 2.0 * sine * sine
-    decay = jnp.exp(-0.005 * radius)
+        doubled = sine + sine
+        sine, cosine = doubled * cosine, 1.0 - doubled * sine
+    decay = jnp.exp2((-0.005 * math.log2(math.e)) * radius)
     return inverse, decay * cosine, decay * sine
 
 
@@ -129,7 +130,7 @@
         picked[:, at] = pick_coefficients(coef[...], body[:, at])
         return carry
 
-    lax.fori_loop(0, blocks, pick, 0)
+    lax.fori_loop(0, blocks, pick, 0, unroll=True)
 
     def half(row_at, start):
         at = pl.ds(pl.multiple_of(start, LANES), LANES)
@@ -271,7 +272,7 @@
     held = [pltpu.VMEM(inputs[i].shape, inputs[i].dtype) for i in range(6)]
     scale = 1.0 / (2.0 * rows * n_tgt)
     return pl.pallas_call(
-        functools.partial(sketch_kernel, max(own, math.gcd(rows, 64)), 2 * LANES, n_src, n_tgt, scale),
+        functools.partial(sketch_kernel, max(own, math.gcd(rows, 64)), 4 * LANES, n_src, n_tgt, scale),
         out_shape=(
             jax.ShapeDtypeStruct((2 * own, rank_width), jnp.float32),
             jax.ShapeDtypeStruct((rank_width, rank_width), jnp.float32),
@@ -304,7 +305,7 @@
     columns_at = lax.broadcasted_iota(jnp.int32, (size, size), 1)
     work[:, :size] = gram[...]
     work[:, size:] = jnp.where(rows_at == columns_at, 1.0, 0.0)
-    depth = 8
+    depth = 32
     sub = lax.broadcasted_iota(jnp.int32, (depth, size), 0)
 
     def row_of(block, index):
@@ -324,7 +325,7 @@
             pivots = pivot if pivots is None else jnp.where(sub >= k, pivot, pivots)
             if k == depth - 1:
                 break
-            ratio = jnp.where(sub > k, columns[k] / pivot, 0.0)
+            ratio = jnp.where(sub > k, columns[k], 0.0) * (1.0 / pivot)
             for c in range(k + 1, depth):
                 columns[c] = columns[c] - ratio * row_of(columns[c], k)
             left = left - ratio * row_of(left, k)

time: 72.6 us -> 67 us (0.923)
  Pallas kernels: 71.8 us -> 66.2 us
    pallas_call x1, Pallas kernels: 9.93 us -> 6 us  [orthonormalize(): pl.pallas_call(functools.partial(factor_kernel, own), out_shape=(jax.Shap...]
    pallas_call x1, Pallas kernels: 61.9 us -> 60.2 us  [sketch(): pl.pallas_call(functools.partial(sketch_kernel, max(own, math.gcd(rows, 6...]
where the time goes in v3:
time: 67 us; the launch traced here: 66.8 us
  Pallas kernels  66.2 us (99%)
    pallas_call x1, Pallas kernels, sketch(): pl.pallas_call(functools.partial(sketch_kernel, max(own, math.gcd(rows, 6...  60.2 us
    pallas_call x1, Pallas kernels, orthonormalize(): pl.pallas_call(functools.partial(factor_kernel, own), out_shape=(jax.Shap...  6 us

profile of v3, /device:TPU:0, one launch (start us, length us, event | category | flops | bytes accessed | tf_op | source)
XLA Modules:
  0.0 66.8 jit_solution(9066937231610323799)
XLA Ops:
  0.6 60.2 %sketch.1 = (f32[128,128]{1,0:T(8,128)}, f32[128,128]{1,0:T(8,128)}) custom-call(f32[2,512]{1,0:T(2,128)} %txy_in.1, f32[2,2048]{1,0:T(2,128)} %sxy_in.1, s32[1,2048]{1,0:T(1,128)} %bitcast.4, f32[64,128]{1,0:T(8,128)} %bitcast.3, bf16[2048,128]{1,0:T(8,128)(2,1)} %probe_in.1, f32[1,512]{1,0:T(1,128)} %bitcast.5), custom_call_target="tpu_custom_call" | custom-call | tf_op jit(solution)/shard_map/sketch/pallas_call | solution.py:274
  60.8 6.0 %orthonormalize.1 = (f32[64,256]{1,0:T(8,128)}, f32[128,128]{1,0:T(8,128)}) custom-call(f32[128,128]{1,0:T(8,128)} %get-tuple-element.4.stacked, f32[128,128]{1,0:T(8,128)} %get-tuple-element.5.gram), custom_call_target="tpu_custom_call" | custom-call | tf_op jit(solution)/shard_map/orthonormalize/pallas_call | solution.py:354

commit v4 on v3

--- a/solution.py
+++ b/solution.py
@@ -89,13 +89,6 @@
     tgt_me = lax.axis_index("tgt")
     src_peers = [lax.rem(src_me + offset, n_src) for offset in range(1, n_src)]
     tgt_peers = [lax.rem(tgt_me + offset, n_tgt) for offset in range(1, n_tgt)]
-    barrier = pltpu.get_barrier_semaphore()
-    for axis, peers in (("src", src_peers), ("tgt", tgt_peers)):
-        for peer in peers:
-            pl.semaphore_signal(
-                barrier, inc=1, device_id={axis: peer}, device_id_type=pl.DeviceIdType.MESH
-            )
-
     loads = [
         pltpu.make_async_copy(start, end, in_sem.at[index])
         for index, (start, end) in enumerate(
@@ -105,8 +98,12 @@
     ]
     for load in loads:
         load.start()
-    for load in loads:
-        load.wait()
+    barrier = pltpu.get_barrier_semaphore()
+    for axis, peers in (("src", src_peers), ("tgt", tgt_peers)):
+        for peer in peers:
+            pl.semaphore_signal(
+                barrier, inc=1, device_id={axis: peer}, device_id_type=pl.DeviceIdType.MESH
+            )
 
     rows = txy.shape[1]
     sources = sxy.shape[1]
@@ -119,6 +116,8 @@
     piece = piece_mine.shape[0]
     owners = rank_width // piece
 
+    loads[0].wait()
+    loads[4].wait()
     for axis in range(3):
         for start in range(0, rows, LANES):
             at = slice(start, start + LANES)
@@ -130,7 +129,11 @@
         picked[:, at] = pick_coefficients(coef[...], body[:, at])
         return carry
 
+    loads[2].wait()
+    loads[3].wait()
     lax.fori_loop(0, blocks, pick, 0, unroll=True)
+    loads[1].wait()
+    loads[5].wait()
 
     def half(row_at, start):
         at = pl.ds(pl.multiple_of(start, LANES), LANES)
@@ -206,7 +209,6 @@
     own_weight = spread[2, own_at, :]
     stacked = jnp.concatenate(
         [total[:, :rank_width] * own_weight, total[:, rank_width:] * own_weight], axis=0)
-    stacked_out[...] = stacked
     gram_mine[...] = lax.dot_general(
         stacked, stacked, (((0,), (0,)), ((), ())),
         precision=lax.Precision.HIGHEST, preferred_element_type=jnp.float32)
@@ -251,6 +253,7 @@
         for copy in copies + sends:
             copy.wait_send()
 
+    stacked_out[...] = stacked
     guarded(mine, some_idle, merge)
     for peer in src_peers:
         guarded(peer < owners, some_idle, lambda peer=peer: remote(

time: 67 us -> 66.8 us (level)
  no operation moved by 1% of the time
where the time goes in v4:
time: 66.8 us; the launch traced here: 66.6 us
  Pallas kernels  66 us (99%)
    pallas_call x1, Pallas kernels, sketch(): pl.pallas_call(functools.partial(sketch_kernel, max(own, math.gcd(rows, 6...  60 us
    pallas_call x1, Pallas kernels, orthonormalize(): pl.pallas_call(functools.partial(factor_kernel, own), out_shape=(jax.Shap...  6 us

profile of v4, /device:TPU:0, one launch (start us, length us, event | category | flops | bytes accessed | tf_op | source)
XLA Modules:
  0.0 66.6 jit_solution(10156714042817685496)
XLA Ops:
  0.6 60.0 %sketch.1 = (f32[128,128]{1,0:T(8,128)}, f32[128,128]{1,0:T(8,128)}) custom-call(f32[2,512]{1,0:T(2,128)} %txy_in.1, f32[2,2048]{1,0:T(2,128)} %sxy_in.1, s32[1,2048]{1,0:T(1,128)} %bitcast.4, f32[64,128]{1,0:T(8,128)} %bitcast.3, bf16[2048,128]{1,0:T(8,128)(2,1)} %probe_in.1, f32[1,512]{1,0:T(1,128)} %bitcast.5), custom_call_target="tpu_custom_call" | custom-call | tf_op jit(solution)/shard_map/sketch/pallas_call | solution.py:277
  60.6 6.0 %orthonormalize.1 = (f32[64,256]{1,0:T(8,128)}, f32[128,128]{1,0:T(8,128)}) custom-call(f32[128,128]{1,0:T(8,128)} %get-tuple-element.4.stacked, f32[128,128]{1,0:T(8,128)} %get-tuple-element.5.gram), custom_call_target="tpu_custom_call" | custom-call | tf_op jit(solution)/shard_map/orthonormalize/pallas_call | solution.py:357
